TPU v7x, 256 devices: a whole 4x4x8 slice. The times are simulated.
256 devices in a mesh: gx: 8 (over z), gz: 16 (over x, y), col: 2 (over core).
Axes of the slice: x: 4, y: 4, z: 8, core: 2. Of those that a mesh axis runs over, the one named last changes fastest.
Arguments:
- density: float32 [256, 256, 256], P('gx', 'gz', 'col'), may hold values from 0.5 to 2
- momentum: float32 [3, 256, 256, 256], P(None, 'gx', 'gz', 'col'), may hold values from -6 to 6
- adjoint: float32 [5, 256, 256, 256], P(None, 'gx', 'gz', 'col'), may hold values from -6 to 6
- objective: float32 [5, 256, 256, 256], P(None, 'gx', 'gz', 'col'), may hold values from -6 to 6
- flux_jac: float32 [3, 5, 5], replicated, may hold values from -2.5 to 2.5
- wall_owner: int32 [2097152, 1], P(('gx', 'gz', 'col')), may hold values from 0 to 255; in each aligned block of 8192 rows (0 to 8191, 8192 to 16383, ...) at most 64 rows name the same one
- wall_node: int32 [2097152], P(('gx', 'gz', 'col')), may hold values from 0 to 8191
- wall_cell: int32 [2097152], P(('gx', 'gz', 'col')), may hold values from 0 to 65535
- wall_weight: float32 [2097152], P(('gx', 'gz', 'col')), may hold values from 0.5 to 2
- wall_normal: float32 [3, 2097152], P(None, ('gx', 'gz', 'col')), may hold values from -6 to 6
- shell_source: float32 [3, 2097152], P(None, ('gx', 'gz', 'col')), may hold values from -6 to 6
- shell_diag: float32 [3, 2097152], P(None, ('gx', 'gz', 'col')), may hold values from 0.5 to 2
- shell_coupling: float32 [3, 3, 2097152], P(None, None, ('gx', 'gz', 'col')), may hold values from -4 to 4
Outputs:
- fluid_out: float32 [5, 256, 256, 256], P(None, 'gx', 'gz', 'col')
- shell_adjoint: float32 [3, 2097152], P(None, ('gx', 'gz', 'col'))
Inputs may be any that keep to these rules, and one draw needn't show every extreme that they name: `wall_owner`: at most 64 of the rows of one device name the same owner.
All inputs are finite; a program needn't handle non-finite values.
Results may differ from a plain program's by a relative error of at most 0.00011.
Values sent between devices are 32-bit elements; how exact they have to be, the bound alone decides.
A program may use at most 128 MiB of HBM per device.

v0:
```python
import functools

import jax
import jax.numpy as jnp
from jax import lax
from jax.experimental import pallas as pl
from jax.experimental.pallas import tpu as pltpu
from jax.sharding import PartitionSpec as P

tau = 0.25
f32, bf16, i32 = jnp.float32, jnp.bfloat16, jnp.int32
MESH = pl.DeviceIdType.MESH
GX, GZ, COL = 8, 16, 2
CX, CZ, SP = 32, 16, 128
FACES, NODES = 8192, 8192
CHUNK = 1024
VMEM_LIMIT = 56 * 1024 * 1024


def vmem():
    return pl.BlockSpec(memory_space=pltpu.VMEM)


def split(x):
    high = x.astype(bf16).astype(f32)
    return high, x - high


def one_hot(rows, index):
    return lax.broadcasted_iota(i32, (rows, index.shape[1]), 0) == index


def as_bf16(mask):
    return jnp.where(mask, 1.0, 0.0).astype(bf16)


def dot(a, b):
    return jnp.dot(a, b, preferred_element_type=f32)


def dot_nt(a, b):
    return lax.dot_general(a, b, (((1,), (1,)), ((), ())), preferred_element_type=f32)


def owner_column(owner):
    return (owner % 2) * 128 + owner // 2


def slots_from(summed):
    return jnp.concatenate([summed[:, :128], summed[:, 128:]], 0).T


def order_kernel(owner_ref, node_ref, weight_ref, normal_ref, rank_ref, pay_ref, owners_ref, carry_ref, acc_ref):
    rows = lax.broadcasted_iota(i32, (256, 384), 0)
    cols = lax.broadcasted_iota(i32, (256, 384), 1)
    ahead = as_bf16((rows < cols) | (cols >= 256))
    carry_ref[...] = jnp.zeros_like(carry_ref)
    acc_ref[...] = jnp.zeros_like(acc_ref)

    def rank_step(block, _):
        at = pl.ds(pl.multiple_of(block * 256, 256), 256)
        mask = one_hot(256, owner_column(owner_ref[:, at]))
        chosen = as_bf16(mask)
        owners_ref[:, at] = chosen
        counts = dot(chosen, ahead)
        carry = carry_ref[...]
        before = counts[:, :256] + jnp.concatenate([carry, carry], 1)
        rank_ref[:, at] = jnp.sum(jnp.where(mask, before, 0.0), 0, keepdims=True).astype(i32)
        carry_ref[...] = carry + counts[:, 256:]
        return 0

    lax.fori_loop(0, FACES // 256, rank_step, 0)

    def place_step(block, _):
        at = pl.ds(pl.multiple_of(block * CHUNK, CHUNK), CHUNK)
        within = one_hot(64, rank_ref[:, at])
        weight = weight_ref[:, at]
        node = node_ref[:, at]
        pieces = []
        for k in range(3):
            pieces += split(weight * normal_ref[k : k + 1, at])
        pieces += [((node // 128) * 128).astype(f32), (node % 128).astype(f32)]
        stacked = jnp.concatenate(
            [jnp.where(within, piece, 0.0).astype(bf16) for piece in pieces], 0
        )
        acc_ref[...] += dot_nt(stacked, owners_ref[:, at])
        return 0

    lax.fori_loop(0, FACES // CHUNK, place_step, 0)
    for k in range(4):
        pay_ref[k] = slots_from(
            acc_ref[k * 128 : k * 128 + 64, :] + acc_ref[k * 128 + 64 : k * 128 + 128, :]
        )


def order(owner, node, weight, normal):
    return pl.pallas_call(
        order_kernel,
        out_shape=(
            jax.ShapeDtypeStruct((1, FACES), i32),
            jax.ShapeDtypeStruct((4, 128, 128), f32),
        ),
        in_specs=[vmem()] * 4,
        out_specs=(vmem(), vmem()),
        scratch_shapes=[
            pltpu.VMEM((256, FACES), bf16),
            pltpu.VMEM((256, 128), f32),
            pltpu.VMEM((512, 256), f32),
        ],
        compiler_params=pltpu.CompilerParams(vmem_limit_bytes=VMEM_LIMIT),
        name="order",
    )(owner, node, weight, normal)


def place():
    return lax.axis_index("gx"), lax.axis_index("gz"), lax.axis_index("col")


def greet(gx, gz, col):
    barrier = pltpu.get_barrier_semaphore()
    for k in range(1, GX):
        pl.semaphore_signal(barrier, inc=1, device_id=((gx + k) % GX, gz, col), device_id_type=MESH)
    for k in range(1, GZ):
        pl.semaphore_signal(barrier, inc=1, device_id=(gx, (gz + k) % GZ, col), device_id_type=MESH)
    pl.semaphore_signal(barrier, inc=1, device_id=(gx, gz, 1 - col), device_id_type=MESH)
    pl.semaphore_wait(barrier, GX + GZ - 1)


def remote(src, dst, sems, k, device):
    return pltpu.make_async_remote_copy(
        src_ref=src,
        dst_ref=dst,
        send_sem=sems.at[0, k],
        recv_sem=sems.at[1, k],
        device_id=device,
        device_id_type=MESH,
    )


def run(copies, local):
    for copy in copies:
        copy.start()
    local.start()
    for copy in copies:
        copy.wait_recv()
    local.wait()


def drain(copies):
    for copy in copies:
        copy.wait_send()


def exchange_kernel(lead, with_halo, forward, *refs):
    gx, gz, col = place()
    every = (slice(None),) * lead
    if with_halo:
        pay, adjoint, second, third, xlo, xhi, zlo, zhi, side, first, sems_z, sems_g, sems_c, local, sems_h = refs
    elif forward:
        pay, second, third, first, sems_z, sems_g, sems_c, local = refs
    else:
        answers, back, other, mixed, first, sems_z, sems_g, sems_c, local = refs
    greet(gx, gz, col)
    started = []
    sibling = (gx, gz, 1 - col)
    if with_halo:
        up, down = ((gx + 1) % GX, gz, col), ((gx + GX - 1) % GX, gz, col)
        high, low = (gx, (gz + 1) % GZ, col), (gx, (gz + GZ - 1) % GZ, col)
        halos = [
            remote(adjoint.at[:, CX - 2 : CX], xlo, sems_h, 0, up),
            remote(adjoint.at[:, 0:2], xhi, sems_h, 1, down),
            remote(adjoint.at[:, :, CZ - 2 : CZ], zlo, sems_h, 2, high),
            remote(adjoint.at[:, :, 0:2], zhi, sems_h, 3, low),
            remote(adjoint, side, sems_h, 4, sibling),
        ]
        for copy in halos:
            copy.start()
        started += halos
    if forward:
        copies = [
            remote(
                pay.at[every + ((gx + k) % GX,)], first.at[(gx,) + every], sems_z, k - 1, ((gx + k) % GX, gz, col)
            )
            for k in range(1, GX)
        ]
        run(copies, pltpu.make_async_copy(pay.at[every + (gx,)], first.at[(gx,) + every], local.at[0]))
        started += copies
        rows = (slice(None),) * (lead + 1)
        copies = [
            remote(
                first.at[rows + ((gz + k) % GZ,)], second.at[gz], sems_g, k - 1, (gx, (gz + k) % GZ, col)
            )
            for k in range(1, GZ)
        ]
        run(copies, pltpu.make_async_copy(first.at[rows + (gz,)], second.at[gz], local.at[1]))
        started += copies
        copy = remote(second, third, sems_c, 0, sibling)
        copy.start()
        copy.wait_recv()
        started += [copy]
    else:
        copy = remote(answers, other, sems_c, 0, sibling)
        copy.start()
        copy.wait_recv()
        started += [copy]
        half = lax.broadcasted_iota(i32, (GZ * GX, 128), 1) // 64
        mixed[...] = jnp.where(
            half == col,
            answers[...].reshape(GZ * GX, 128),
            pltpu.roll(other[...].reshape(GZ * GX, 128), 64, 1),
        ).reshape(GZ, GX, 128)
        copies = [
            remote(mixed.at[(gz + k) % GZ], first.at[:, gz], sems_g, k - 1, (gx, (gz + k) % GZ, col))
            for k in range(1, GZ)
        ]
        run(copies, pltpu.make_async_copy(mixed.at[gz], first.at[:, gz], local.at[1]))
        started += copies
        copies = [
            remote(first.at[(gx + k) % GX], back.at[gx], sems_z, k - 1, ((gx + k) % GX, gz, col))
            for k in range(1, GX)
        ]
        run(copies, pltpu.make_async_copy(first.at[gx], back.at[gx], local.at[0]))
        started += copies
    if with_halo:
        for copy in halos:
            copy.wait_recv()
    drain(started)


def semaphores(with_halo=False):
    dma = pltpu.SemaphoreType.DMA
    return [dma((2, GX - 1)), dma((2, GZ - 1)), dma((2, 1)), dma((2,))] + ([dma((2, 5))] if with_halo else [])


def comm_call(kernel, args, out_shapes, scratch, collective_id, name):
    return pl.pallas_call(
        kernel,
        out_shape=tuple(jax.ShapeDtypeStruct(shape, f32) for shape in out_shapes),
        in_specs=[vmem()] * len(args),
        out_specs=tuple(vmem() for _ in out_shapes),
        scratch_shapes=scratch,
        compiler_params=pltpu.CompilerParams(
            collective_id=collective_id, has_side_effects=True, vmem_limit_bytes=VMEM_LIMIT
        ),
        name=name,
    )(*args)


def exchange_first(pay, adjoint):
    return comm_call(
        functools.partial(exchange_kernel, 1, True, True),
        (pay, adjoint),
        [(GZ, GX, 4, 128)] * 2 + [(5, 2, CZ, SP)] * 2 + [(5, CX, 2, SP)] * 2 + [(5, CX, CZ, SP)],
        [pltpu.VMEM((GX, 4, GZ, 128), f32)] + semaphores(True),
        0,
        "exchange_first",
    )


def exchange_pressure(pay):
    return comm_call(
        functools.partial(exchange_kernel, 0, False, True),
        (pay,),
        [(GZ, GX, 128)] * 2,
        [pltpu.VMEM((GX, GZ, 128), f32)] + semaphores(),
        1,
        "exchange_pressure",
    )


def exchange_back(answers):
    return comm_call(
        functools.partial(exchange_kernel, 0, False, False),
        (answers,),
        [(GX, GZ, 128)],
        [pltpu.VMEM((GZ, GX, 128), f32), pltpu.VMEM((GZ, GX, 128), f32), pltpu.VMEM((GX, GZ, 128), f32)] + semaphores(),
        2,
        "exchange_back",
    )[0]


def fluid_kernel(
    flux, density, momentum, adjoint, objective, xlo, xhi, zlo, zhi, side,
    owner_ref, rank_ref, cell_ref, middle, plane_ref, pay_ref, ext, wide, acc_ref,
):
    gx, gz, col = place()
    lane = lax.broadcasted_iota(i32, (CZ, SP), 1)
    x_low = (gx > 0).astype(f32)
    x_high = (gx < GX - 1).astype(f32)
    z_low = (gz > 0).astype(f32)
    z_high = (gz < GZ - 1).astype(f32)
    s_low = (col > 0).astype(f32)
    s_high = (col < COL - 1).astype(f32)
    for j in range(5):
        ext[j, 2 : CX + 2] = adjoint[j]
        ext[j, 0:2] = xlo[j] * x_low
        ext[j, CX + 2 : CX + 4] = xhi[j] * x_high

    def plane_step(x, _):
        inverse = (tau / 12.0) / density[x]
        velocity = [momentum[d, x] * inverse for d in range(3)]
        deltas = []
        for j in range(5):
            here = adjoint[j, x]
            beside = side[j, x]
            dx = 8.0 * (ext[j, x + 1] - ext[j, x + 3]) - (ext[j, x] - ext[j, x + 4])
            tall = jnp.concatenate([zlo[j, x] * z_low, here, zhi[j, x] * z_high], 0)
            dz = 8.0 * (tall[1:17] - tall[3:19]) - (tall[0:16] - tall[4:20])
            low_side, high_side = beside * s_low, beside * s_high
            ds = 8.0 * (
                pltpu.roll(jnp.where(lane >= SP - 1, low_side, here), 1, 1)
                - pltpu.roll(jnp.where(lane < 1, high_side, here), SP - 1, 1)
            ) - (
                pltpu.roll(jnp.where(lane >= SP - 2, low_side, here), 2, 1)
                - pltpu.roll(jnp.where(lane < 2, high_side, here), SP - 2, 1)
            )
            deltas.append((dx, dz, ds))
        for i in range(5):
            total = velocity[0] * deltas[i][0] + velocity[1] * deltas[i][1] + velocity[2] * deltas[i][2]
            for d in range(3):
                for j in range(5):
                    total = total + (flux[d * 25 + j * 5 + i] * (tau / 12.0)) * deltas[j][d]
            value = adjoint[i, x] - (total + tau * objective[i, x])
            middle[i, x] = value
            if i == 4:
                plane_ref[pl.ds(pl.multiple_of(x * CZ, CZ), CZ), :] = value
        return 0

    lax.fori_loop(0, CX, plane_step, 0)

    turned = plane_ref[...].T
    high, low = split(turned)
    wide[0:128, :] = high.astype(bf16)
    wide[128:256, :] = low.astype(bf16)
    acc_ref[...] = jnp.zeros_like(acc_ref)

    def face_step(block, _):
        at = pl.ds(pl.multiple_of(block * CHUNK, CHUNK), CHUNK)
        cell = cell_ref[:, at]
        picked = dot(wide[...], as_bf16(one_hot(CX * CZ, cell // SP)))
        across = one_hot(SP, cell % SP)
        first = jnp.sum(jnp.where(across, picked[:128], 0.0), 0, keepdims=True)
        second = jnp.sum(jnp.where(across, picked[128:], 0.0), 0, keepdims=True)
        within = one_hot(64, rank_ref[:, at])
        stacked = jnp.concatenate(
            [jnp.where(within, first, 0.0).astype(bf16), jnp.where(within, second, 0.0).astype(bf16)], 0
        )
        acc_ref[...] += dot_nt(stacked, as_bf16(one_hot(256, owner_column(owner_ref[:, at]))))
        return 0

    lax.fori_loop(0, FACES // CHUNK, face_step, 0)
    pay_ref[...] = slots_from(acc_ref[0:64, :] + acc_ref[64:128, :]).reshape(GX, GZ, 128)


def fluid(flux, density, momentum, adjoint, objective, halos, owner, rank, cell):
    return pl.pallas_call(
        fluid_kernel,
        out_shape=(
            jax.ShapeDtypeStruct((5, CX, CZ, SP), f32),
            jax.ShapeDtypeStruct((CX * CZ, SP), f32),
            jax.ShapeDtypeStruct((GX, GZ, 128), f32),
        ),
        in_specs=[pl.BlockSpec(memory_space=pltpu.SMEM)] + [vmem()] * 12,
        out_specs=(vmem(),) * 3,
        scratch_shapes=[
            pltpu.VMEM((5, CX + 4, CZ, SP), f32),
            pltpu.VMEM((256, 512), bf16),
            pltpu.VMEM((128, 256), f32),
        ],
        compiler_params=pltpu.CompilerParams(vmem_limit_bytes=VMEM_LIMIT),
        name="fluid",
    )(flux, density, momentum, adjoint, objective, *halos, owner, rank, cell)


def shell_kernel(
    fixed_own, fixed_other, press_own, press_other, source, diag, coupling,
    shell_ref, answer_ref, fixed, press, rows_ref, table, acc_ref,
):
    col = lax.axis_index("col")
    half = lax.broadcasted_iota(i32, (GX, 4, 128), 2) // 64
    half_p = lax.broadcasted_iota(i32, (GX, 128), 1) // 64
    for g in range(GZ):
        other = fixed_other[g]
        fixed[g] = jnp.where(half == col, fixed_own[g], pltpu.roll(other, 64, 2))
        press[g] = jnp.where(half_p == col, press_own[g], pltpu.roll(press_other[g], 64, 1))
    acc_ref[...] = jnp.zeros_like(acc_ref)

    def row(g, k):
        return jnp.concatenate([fixed[g, x, k : k + 1, :] for x in range(GX)], 1)

    def add_step(g, _):
        node = row(g, 3).astype(i32)
        line = node // 128
        rows = as_bf16(one_hot(256, (line // 32) * 128 + node % 128))
        rows_ref[g] = rows
        columns = one_hot(32, line % 32)
        pressure = jnp.concatenate([press[g, x : x + 1, :] for x in range(GX)], 1)
        pieces = []
        for k in range(3):
            pieces += split(pressure * row(g, k))
        stacked = jnp.concatenate([jnp.where(columns, piece, 0.0).astype(bf16) for piece in pieces], 0)
        acc_ref[...] += dot_nt(stacked, rows)
        return 0

    lax.fori_loop(0, GZ, add_step, 0)
    loads = []
    for k in range(3):
        both = acc_ref[k * 64 : k * 64 + 32, :] + acc_ref[k * 64 + 32 : k * 64 + 64, :]
        loads.append(jnp.concatenate([both[:, :128], both[:, 128:]], 0) + source[:, k, :])
    for i in range(3):
        value = diag[:, i, :] * loads[i]
        for j in range(3):
            value = value + coupling[i, :, j, :] * loads[j]
        shell_ref[:, i, :] = value
        wide = jnp.concatenate([value[0:32], value[32:64]], 1)
        high, low = split(wide)
        table[i * 64 : i * 64 + 32, :] = high.astype(bf16)
        table[i * 64 + 32 : i * 64 + 64, :] = low.astype(bf16)

    def pick_step(g, _):
        picked = dot(table[...], rows_ref[g])
        node = row(g, 3).astype(i32)
        columns = one_hot(32, (node // 128) % 32)
        answer = jnp.zeros((1, GX * 128), f32)
        for k in range(3):
            both = picked[k * 64 : k * 64 + 32] + picked[k * 64 + 32 : k * 64 + 64]
            answer = answer + row(g, k) * jnp.sum(jnp.where(columns, both, 0.0), 0, keepdims=True)
        for x in range(GX):
            answer_ref[g, x : x + 1, :] = answer[:, x * 128 : x * 128 + 128]
        return 0

    lax.fori_loop(0, GZ, pick_step, 0)


def shell_part(fixed_own, fixed_other, press_own, press_other, source, diag, coupling):
    return pl.pallas_call(
        shell_kernel,
        out_shape=(
            jax.ShapeDtypeStruct((64, 3, 128), f32),
            jax.ShapeDtypeStruct((GZ, GX, 128), f32),
        ),
        in_specs=[vmem()] * 7,
        out_specs=(vmem(),) * 2,
        scratch_shapes=[
            pltpu.VMEM((GZ, GX, 4, 128), f32),
            pltpu.VMEM((GZ, GX, 128), f32),
            pltpu.VMEM((GZ, 256, GX * 128), bf16),
            pltpu.VMEM((192, 256), bf16),
            pltpu.VMEM((192, 256), f32),
        ],
        compiler_params=pltpu.CompilerParams(vmem_limit_bytes=VMEM_LIMIT),
        name="shell",
    )(fixed_own, fixed_other, press_own, press_other, source, diag, coupling)


def update_kernel(back, owner_ref, rank_ref, cell_ref, plane_ref, middle, out, wide, acc_ref, result, sem):
    turned = back[...].reshape(128, 128).T
    high, low = split(jnp.concatenate([turned[0:64], turned[64:128]], 1))
    wide[0:64, :] = high.astype(bf16)
    wide[64:128, :] = low.astype(bf16)
    acc_ref[...] = jnp.zeros_like(acc_ref)

    def face_step(block, _):
        at = pl.ds(pl.multiple_of(block * CHUNK, CHUNK), CHUNK)
        picked = dot(wide[...], as_bf16(one_hot(256, owner_column(owner_ref[:, at]))))
        within = one_hot(64, rank_ref[:, at])
        value = jnp.sum(jnp.where(within, picked[:64] + picked[64:], 0.0), 0, keepdims=True)
        first, second = split(value)
        cell = cell_ref[:, at]
        across = one_hot(SP, cell % SP)
        stacked = jnp.concatenate(
            [jnp.where(across, first, 0.0).astype(bf16), jnp.where(across, second, 0.0).astype(bf16)], 0
        )
        acc_ref[...] += dot_nt(as_bf16(one_hot(CX * CZ, cell // SP)), stacked)
        return 0

    lax.fori_loop(0, FACES // CHUNK, face_step, 0)
    result[...] = (plane_ref[...] + acc_ref[:, :128] + acc_ref[:, 128:]).reshape(CX, CZ, SP)
    copy = pltpu.make_async_copy(result, out.at[4], sem)
    copy.start()
    copy.wait()


def update(back, owner, rank, cell, plane, middle):
    return pl.pallas_call(
        update_kernel,
        out_shape=jax.ShapeDtypeStruct((5, CX, CZ, SP), f32),
        in_specs=[vmem()] * 5 + [pl.BlockSpec(memory_space=pl.ANY)],
        out_specs=pl.BlockSpec(memory_space=pl.ANY),
        input_output_aliases={5: 0},
        scratch_shapes=[
            pltpu.VMEM((128, 256), bf16),
            pltpu.VMEM((512, 256), f32),
            pltpu.VMEM((CX, CZ, SP), f32),
            pltpu.SemaphoreType.DMA,
        ],
        compiler_params=pltpu.CompilerParams(vmem_limit_bytes=VMEM_LIMIT),
        name="update",
    )(back, owner, rank, cell, plane, middle)


def body(
    density, momentum, adjoint, objective, flux_jac, wall_owner, wall_node, wall_cell,
    wall_weight, wall_normal, shell_source, shell_diag, shell_coupling,
):
    owner = wall_owner.reshape(1, FACES)
    node = wall_node.reshape(1, FACES)
    cell = wall_cell.reshape(1, FACES)
    weight = wall_weight.reshape(1, FACES)
    flux = flux_jac.reshape(75)
    source = shell_source.reshape(3, 64, 128).transpose(1, 0, 2)
    diag = shell_diag.reshape(3, 64, 128).transpose(1, 0, 2)
    coupling = shell_coupling.reshape(3, 3, 64, 128).transpose(0, 2, 1, 3)
    rank, pay = order(owner, node, weight, wall_normal)
    fixed_own, fixed_other, *halos = exchange_first(pay.reshape(4, GX, GZ, 128), adjoint)
    middle, plane, pay = fluid(flux, density, momentum, adjoint, objective, halos, owner, rank, cell)
    press_own, press_other = exchange_pressure(pay)
    shell, answers = shell_part(fixed_own, fixed_other, press_own, press_other, source, diag, coupling)
    back = exchange_back(answers)
    fluid_out = update(back, owner, rank, cell, plane, middle)
    return fluid_out, shell.transpose(1, 0, 2).reshape(3, NODES)


def solution(mesh):
    wall = ("gx", "gz", "col")
    return jax.shard_map(
        body,
        mesh=mesh,
        in_specs=(
            P(*wall),
            P(None, *wall),
            P(None, *wall),
            P(None, *wall),
            P(),
            P(wall, None),
            P(wall),
            P(wall),
            P(wall),
            P(None, wall),
            P(None, wall),
            P(None, wall),
            P(None, None, wall),
        ),
        out_specs=(P(None, *wall), P(None, wall)),
        check_vma=False,
    )
```

profile of v0, /device:TPU:8, one launch (start us, length us, event | category | flops | bytes accessed | tf_op | source)
XLA Modules:
  0.0 112.1 jit_solution(3368034886476566479)
XLA Ops:
  0.6 0.7 copy.17
  1.3 0.7 reshape.38.flux
  2.0 14.1 %order.1 = (s32[1,8192]{1,0:T(1,128)}, f32[4,128,128]{2,1,0:T(8,128)}) custom-call(s32[1,8192]{1,0:T(1,128)} %bitcast.18, s32[1,8192]{1,0:T(1,128)} %bitcast.26, f32[1,8192]{1,0:T(1,128)} %bitcast.27, f32[3,8192]{1,0:T(4,128)} %normal_ref.1), custom_call_target="tpu_custom_call" | custom-call | tf_op jit(solution)/shard_map/order/pallas_call | solution.py:97
  16.2 28.4 %exchange_first.1 = (f32[16,8,4,128]{3,2,1,0:T(4,128)}, f32[16,8,4,128]{3,2,1,0:T(4,128)}, f32[5,2,16,128]{3,2,1,0:T(8,128)}, f32[5,2,16,128]{3,2,1,0:T(8,128)},...) custom-call(f32[4,8,16,128]{3,2,1,0:T(8,128)} %bitcast.21, ...), custom_call_target="tpu_custom_call" | custom-call | tf_op jit(solution)/shard_map/exchange_first/pallas_call | solution.py:236
  44.5 14.1 %fluid.1 = (f32[5,32,16,128]{3,2,1,0:T(8,128)}, f32[512,128]{1,0:T(8,128)}, f32[8,16,128]{2,1,0:T(8,128)}) custom-call(f32[75]{0:T(128)} %reshape.38.flux, f32[32,16,128]{2,1,0:T(8,128)} %density.1, f32[3,32,16,128]{3,2,1,0:T(8,128)} %momentum.1, f32[5,32,16,128]{3,2,1,0:T(8,128)} %adjoint.1, f32[5,32,16,128]{3,2,1,0:T(8,128)} %objective.1, ...), custom_call_target="tpu_custom_call" | custom-call | tf_op jit(solution)/shard_map/fluid/pallas_call | solution.py:356
  58.7 17.6 %exchange_pressure.1 = (f32[16,8,128]{2,1,0:T(8,128)}, f32[16,8,128]{2,1,0:T(8,128)}) custom-call(f32[8,16,128]{2,1,0:T(8,128)} %get-tuple-element.27.refs_0_), custom_call_target="tpu_custom_call" | custom-call | tf_op jit(solution)/shard_map/exchange_pressure/pallas_call | solution.py:236
  76.2 13.8 %shell.1 = (f32[64,3,128]{2,1,0:T(4,128)}, f32[16,8,128]{2,1,0:T(8,128)}) custom-call(f32[16,8,4,128]{3,2,1,0:T(4,128)} %get-tuple-element.19.fixed_own, f32[16,8,4,128]{3,2,1,0:T(4,128)} %get-tuple-element.20.fixed_other, f32[16,8,128]{2,1,0:T(8,128)} %get-tuple-element.28.press_own, f32[16,8,128]{2,1,0:T(8,128)} %get-tuple-element.29.press_other, ...), custom_call_target="tpu_custom_call" | custom-call | tf_op jit(solution)/shard_map/shell/pallas_call | solution.py:436
  90.0 14.5 %exchange_back.1.back = f32[8,16,128]{2,1,0:T(8,128)} custom-call(f32[16,8,128]{2,1,0:T(8,128)} %get-tuple-element.30.refs_0_), custom_call_target="tpu_custom_call" | custom-call | tf_op jit(solution)/shard_map/exchange_back/pallas_call | solution.py:236
  104.5 7.6 %update.1 = f32[5,32,16,128]{3,2,1,0:T(8,128)} custom-call(f32[8,16,128]{2,1,0:T(8,128)} %exchange_back.1.back, s32[1,8192]{1,0:T(1,128)} %bitcast.20, s32[1,8192]{1,0:T(1,128)} %get-tuple-element.26.rank_ref, s32[1,8192]{1,0:T(1,128)} %bitcast.23, f32[512,128]{1,0:T(8,128)} %get-tuple-element.31.plane_ref, ...), custom_call_target="tpu_custom_call", output_to_operand_aliasing={{}: (5, {})} | custom-call | tf_op jit(solution)/shard_map/update/pallas_call | solution.py:485
where the time goes:
time: 113 us; the launch traced here: 112 us
  Pallas kernels  110 us (97%)
  local copies, waits for them, and re-layouts  1.38 us (1%)
    pallas_call x3, Pallas kernels, comm_call(): pl.pallas_call(kernel, out_shape=tuple((jax.ShapeDtypeStruct(shape, f32)...  60.4 us
    pallas_call x1, Pallas kernels, order(): pl.pallas_call(order_kernel, out_shape=(jax.ShapeDtypeStruct((1, FACES),...  14.1 us
    pallas_call x1, Pallas kernels, fluid(): pl.pallas_call(fluid_kernel, out_shape=(jax.ShapeDtypeStruct((5, CX, CZ,...  14.1 us
    pallas_call x1, Pallas kernels, shell_part(): pl.pallas_call(shell_kernel, out_shape=(jax.ShapeDtypeStruct((64, 3, 128)...  13.8 us
    pallas_call x1, Pallas kernels, update(): pl.pallas_call(update_kernel, out_shape=jax.ShapeDtypeStruct((5, CX, CZ,...  7.59 us

commit v1 on v0

v1 whole, which is shorter than its diff:
```python
import functools

import jax
import jax.numpy as jnp
from jax import lax
from jax.experimental import pallas as pl
from jax.experimental.pallas import tpu as pltpu
from jax.sharding import PartitionSpec as P

tau = 0.25
f32, bf16, i32 = jnp.float32, jnp.bfloat16, jnp.int32
MESH = pl.DeviceIdType.MESH
GX, GZ, COL = 8, 16, 2
CX, CZ, SP = 32, 16, 128
FACES, NODES = 8192, 8192
CHUNK = 2048
VMEM_LIMIT = 56 * 1024 * 1024


def vmem():
    return pl.BlockSpec(memory_space=pltpu.VMEM)


def split(x):
    high = x.astype(bf16).astype(f32)
    return high, x - high


def one_hot(rows, index):
    return lax.broadcasted_iota(i32, (rows, index.shape[1]), 0) == index


def as_bf16(mask):
    return jnp.where(mask, 1.0, 0.0).astype(bf16)


def dot(a, b):
    return jnp.dot(a, b, preferred_element_type=f32)


def dot_nt(a, b):
    return lax.dot_general(a, b, (((1,), (1,)), ((), ())), preferred_element_type=f32)


def owner_column(owner):
    return (owner % 2) * 128 + owner // 2


def slots_from(summed):
    return jnp.concatenate([summed[:, :128], summed[:, 128:]], 0).T


def place():
    return lax.axis_index("gx"), lax.axis_index("gz"), lax.axis_index("col")


def greet(gx, gz, col):
    barrier = pltpu.get_barrier_semaphore()
    for k in range(1, GX):
        pl.semaphore_signal(barrier, inc=1, device_id=((gx + k) % GX, gz, col), device_id_type=MESH)
    for k in range(1, GZ):
        pl.semaphore_signal(barrier, inc=1, device_id=(gx, (gz + k) % GZ, col), device_id_type=MESH)
    pl.semaphore_signal(barrier, inc=1, device_id=(gx, gz, 1 - col), device_id_type=MESH)


def greeted():
    pl.semaphore_wait(pltpu.get_barrier_semaphore(), GX + GZ - 1)


def remote(src, dst, sems, k, device):
    return pltpu.make_async_remote_copy(
        src_ref=src,
        dst_ref=dst,
        send_sem=sems.at[0, k],
        recv_sem=sems.at[1, k],
        device_id=device,
        device_id_type=MESH,
    )


class Stage:
    def __init__(self, copies, local=None):
        self.copies, self.local = copies, local

    def start(self):
        for copy in self.copies:
            copy.start()
        if self.local is not None:
            self.local.start()
        return self

    def arrive(self):
        for copy in self.copies:
            copy.wait_recv()
        if self.local is not None:
            self.local.wait()

    def sent(self):
        for copy in self.copies:
            copy.wait_send()


def along_gx(here, source, target, sems, local):
    gx, gz, col = here
    return Stage(
        [
            remote(source((gx + k) % GX), target(gx), sems, k - 1, ((gx + k) % GX, gz, col))
            for k in range(1, GX)
        ],
        pltpu.make_async_copy(source(gx), target(gx), local),
    )


def along_gz(here, source, target, sems, local):
    gx, gz, col = here
    return Stage(
        [
            remote(source((gz + k) % GZ), target(gz), sems, k - 1, (gx, (gz + k) % GZ, col))
            for k in range(1, GZ)
        ],
        pltpu.make_async_copy(source(gz), target(gz), local),
    )


def along_col(here, source, target, sems):
    gx, gz, col = here
    return Stage([remote(source, target, sems, 0, (gx, gz, 1 - col))])


def rank_faces(owner_ref, rank_ref, owners_ref, carry_ref):
    rows = lax.broadcasted_iota(i32, (256, 384), 0)
    cols = lax.broadcasted_iota(i32, (256, 384), 1)
    ahead = as_bf16((rows < cols) | (cols >= 256))
    carry_ref[...] = jnp.zeros_like(carry_ref)

    def step(block, _):
        at = pl.ds(pl.multiple_of(block * CHUNK, CHUNK), CHUNK)
        mask = one_hot(256, owner_column(owner_ref[:, at]))
        chosen = as_bf16(mask)
        owners_ref[:, at] = chosen
        carry = carry_ref[...]
        ranks = []
        for k in range(CHUNK // 256):
            counts = dot(chosen[:, k * 256 : k * 256 + 256], ahead)
            before = counts[:, :256] + jnp.concatenate([carry, carry], 1)
            ranks.append(
                jnp.sum(jnp.where(mask[:, k * 256 : k * 256 + 256], before, 0.0), 0, keepdims=True)
            )
            carry = carry + counts[:, 256:]
        rank_ref[:, at] = jnp.concatenate(ranks, 1).astype(i32)
        carry_ref[...] = carry
        return 0

    lax.fori_loop(0, FACES // CHUNK, step, 0)


def place_fixed(node_ref, weight_ref, normal_ref, rank_ref, owners_ref, acc_ref, pay):
    acc_ref[...] = jnp.zeros_like(acc_ref)

    def step(block, _):
        at = pl.ds(pl.multiple_of(block * CHUNK, CHUNK), CHUNK)
        within = one_hot(64, rank_ref[:, at])
        weight = weight_ref[:, at]
        node = node_ref[:, at]
        pieces = []
        for k in range(3):
            pieces += split(weight * normal_ref[k : k + 1, at])
        pieces += [((node // 128) * 128).astype(f32), (node % 128).astype(f32)]
        stacked = jnp.concatenate(
            [jnp.where(within, piece, 0.0).astype(bf16) for piece in pieces], 0
        )
        acc_ref[...] += dot_nt(stacked, owners_ref[:, at])
        return 0

    lax.fori_loop(0, FACES // CHUNK, step, 0)
    for k in range(4):
        pay[k] = slots_from(
            acc_ref[k * 128 : k * 128 + 64, :] + acc_ref[k * 128 + 64 : k * 128 + 128, :]
        ).reshape(GX, GZ, 128)


def stencil(here, flux, density, momentum, adjoint, objective, xlo, xhi, zlo, zhi, side, middle, plane_ref, ext):
    gx, gz, col = here
    lane = lax.broadcasted_iota(i32, (CZ, SP), 1)
    x_low = (gx > 0).astype(f32)
    x_high = (gx < GX - 1).astype(f32)
    z_low = (gz > 0).astype(f32)
    z_high = (gz < GZ - 1).astype(f32)
    s_low = (col > 0).astype(f32)
    s_high = (col < COL - 1).astype(f32)
    for j in range(5):
        ext[j, 0:2] = xlo[j] * x_low
        ext[j, CX + 2 : CX + 4] = xhi[j] * x_high

    def one_plane(x):
        inverse = (tau / 12.0) / density[x]
        velocity = [momentum[d, x] * inverse for d in range(3)]
        deltas = []
        for j in range(5):
            now = ext[j, x + 2]
            beside = side[j, x]
            dx = 8.0 * (ext[j, x + 1] - ext[j, x + 3]) - (ext[j, x] - ext[j, x + 4])
            tall = jnp.concatenate([zlo[j, x] * z_low, now, zhi[j, x] * z_high], 0)
            dz = 8.0 * (tall[1:17] - tall[3:19]) - (tall[0:16] - tall[4:20])
            low_side, high_side = beside * s_low, beside * s_high
            ds = 8.0 * (
                pltpu.roll(jnp.where(lane >= SP - 1, low_side, now), 1, 1)
                - pltpu.roll(jnp.where(lane < 1, high_side, now), SP - 1, 1)
            ) - (
                pltpu.roll(jnp.where(lane >= SP - 2, low_side, now), 2, 1)
                - pltpu.roll(jnp.where(lane < 2, high_side, now), SP - 2, 1)
            )
            deltas.append((dx, dz, ds))
        for i in range(5):
            total = velocity[0] * deltas[i][0] + velocity[1] * deltas[i][1] + velocity[2] * deltas[i][2]
            for d in range(3):
                for j in range(5):
                    total = total + (flux[j, d, i] * (tau / 12.0)) * deltas[j][d]
            value = ext[i, x + 2] - (total + tau * objective[i, x])
            middle[i, x] = value
            if i == 4:
                plane_ref[pl.ds(pl.multiple_of(x * CZ, CZ), CZ), :] = value

    def step(x, _):
        for k in range(2):
            one_plane(2 * x + k)
        return 0

    lax.fori_loop(0, CX // 2, step, 0)


def gather_pressure(cell_ref, rank_ref, owners_ref, plane_ref, wide, acc_ref, pay):
    high, low = split(plane_ref[...].T)
    wide[0:128, :] = high.astype(bf16)
    wide[128:256, :] = low.astype(bf16)
    acc_ref[0:128, :] = jnp.zeros((128, 256), f32)

    def step(block, _):
        at = pl.ds(pl.multiple_of(block * CHUNK, CHUNK), CHUNK)
        cell = cell_ref[:, at]
        picked = dot(wide[...], as_bf16(one_hot(CX * CZ, cell // SP)))
        across = one_hot(SP, cell % SP)
        first = jnp.sum(jnp.where(across, picked[:128], 0.0), 0, keepdims=True)
        second = jnp.sum(jnp.where(across, picked[128:], 0.0), 0, keepdims=True)
        within = one_hot(64, rank_ref[:, at])
        stacked = jnp.concatenate(
            [jnp.where(within, first, 0.0).astype(bf16), jnp.where(within, second, 0.0).astype(bf16)], 0
        )
        acc_ref[0:128, :] += dot_nt(stacked, owners_ref[:, at])
        return 0

    lax.fori_loop(0, FACES // CHUNK, step, 0)
    pay[...] = slots_from(acc_ref[0:64, :] + acc_ref[64:128, :]).reshape(GX, GZ, 128)


ROWS = GX * GZ * 128


def flat(ref, *tail):
    return lambda g: jnp.concatenate([ref[(g, slice(x, x + 1)) + tail] for x in range(GX)], 1)


def combine(col, own, other):
    half = lax.broadcasted_iota(i32, own.shape, own.ndim - 1) // 64
    return jnp.where(half == col, own, pltpu.roll(other, 64, own.ndim - 1))


def fixed_rows(col, own, other, fixed, rows_ref):
    for g in range(GZ):
        fixed[g] = combine(col, own[g], other[g])

    def step(g, _):
        for k in range(2):
            node = row(fixed, 2 * g + k, 3).astype(i32)
            line = node // 128
            rows_ref[2 * g + k] = as_bf16(one_hot(256, (line // 32) * 128 + node % 128))
        return 0

    lax.fori_loop(0, GZ // 2, step, 0)


def row(fixed, g, k):
    return jnp.concatenate([fixed[g, x, k : k + 1, :] for x in range(GX)], 1)


def node_columns(fixed, g):
    return one_hot(32, (row(fixed, g, 3).astype(i32) // 128) % 32)


def add_loads(press, fixed, rows_ref, acc_ref):
    acc_ref[0:192, :] = jnp.zeros((192, 256), f32)

    def step(h, _):
        total = acc_ref[0:192, :]
        for k in range(2):
            g = 2 * h + k
            columns = node_columns(fixed, g)
            pressure = jnp.concatenate([press[g, x : x + 1, :] for x in range(GX)], 1)
            pieces = []
            for c in range(3):
                pieces += split(pressure * row(fixed, g, c))
            stacked = jnp.concatenate([jnp.where(columns, piece, 0.0).astype(bf16) for piece in pieces], 0)
            total = total + dot_nt(stacked, rows_ref[g])
        acc_ref[0:192, :] = total
        return 0

    lax.fori_loop(0, GZ // 2, step, 0)


def solve_shell(acc_ref, source, diag, coupling, shell_ref, table):
    loads = []
    for k in range(3):
        both = acc_ref[k * 64 : k * 64 + 32, :] + acc_ref[k * 64 + 32 : k * 64 + 64, :]
        loads.append(jnp.concatenate([both[:, :128], both[:, 128:]], 0) + source[:, k, :])
    for i in range(3):
        value = diag[:, i, :] * loads[i]
        for j in range(3):
            value = value + coupling[i, :, j, :] * loads[j]
        shell_ref[:, i, :] = value
        wide = jnp.concatenate([value[0:32], value[32:64]], 1)
        high, low = split(wide)
        table[i * 64 : i * 64 + 32, :] = high.astype(bf16)
        table[i * 64 + 32 : i * 64 + 64, :] = low.astype(bf16)


def pick_answers(table, fixed, rows_ref, answers):
    def step(h, _):
        for k in range(2):
            g = 2 * h + k
            picked = dot(table[...], rows_ref[g])
            columns = node_columns(fixed, g)
            answer = jnp.zeros((1, GX * 128), f32)
            for c in range(3):
                both = picked[c * 64 : c * 64 + 32] + picked[c * 64 + 32 : c * 64 + 64]
                answer = answer + row(fixed, g, c) * jnp.sum(jnp.where(columns, both, 0.0), 0, keepdims=True)
            for x in range(GX):
                answers[g, x : x + 1, :] = answer[:, x * 128 : x * 128 + 128]
        return 0

    lax.fori_loop(0, GZ // 2, step, 0)


def main_kernel(
    owner, node, cell, weight, normal, source, diag, coupling,
    flux_hbm, density_hbm, momentum_hbm, adjoint_hbm, objective_hbm,
    rank, plane, shell, back, middle_hbm,
    flux, density, momentum, objective, ext, middle, xlo, xhi, zlo, zhi, side,
    owners, carry, acc, wide, rows_ref, table,
    pay0, hop0, own0, other0, fixed, pay1, hop1, own1, other1, press, answers, other2, mixed, hop2,
    sems_h, sems_z, sems_g, sems_c, local, loads,
):
    here = gx, gz, col = place()
    greet(gx, gz, col)
    staged = [
        pltpu.make_async_copy(adjoint_hbm, ext.at[:, 2 : CX + 2], loads.at[0]),
        pltpu.make_async_copy(momentum_hbm, momentum, loads.at[1]),
        pltpu.make_async_copy(density_hbm, density, loads.at[2]),
        pltpu.make_async_copy(objective_hbm, objective, loads.at[3]),
        pltpu.make_async_copy(flux_hbm, flux, loads.at[4]),
    ]
    for copy in staged:
        copy.start()
    rank_faces(owner, rank, owners, carry)
    greeted()
    up, down = ((gx + 1) % GX, gz, col), ((gx + GX - 1) % GX, gz, col)
    high, low = (gx, (gz + 1) % GZ, col), (gx, (gz + GZ - 1) % GZ, col)
    halos = Stage(
        [
            remote(adjoint_hbm.at[:, CX - 2 : CX], xlo, sems_h, 0, up),
            remote(adjoint_hbm.at[:, 0:2], xhi, sems_h, 1, down),
            remote(adjoint_hbm.at[:, :, CZ - 2 : CZ], zlo, sems_h, 2, high),
            remote(adjoint_hbm.at[:, :, 0:2], zhi, sems_h, 3, low),
            remote(adjoint_hbm, side, sems_h, 4, (gx, gz, 1 - col)),
        ]
    ).start()
    place_fixed(node, weight, normal, rank, owners, acc, pay0)
    fixed_z = along_gx(here, lambda x: pay0.at[:, x], lambda x: hop0.at[x], sems_z.at[0], local.at[0]).start()
    for copy in staged:
        copy.wait()
    halos.arrive()
    stencil(here, flux, density, momentum, adjoint_hbm, objective, xlo, xhi, zlo, zhi, side, middle, plane, ext)
    write = pltpu.make_async_copy(middle, middle_hbm, loads.at[5])
    write.start()
    fixed_z.arrive()
    fixed_g = along_gz(here, lambda z: hop0.at[:, :, z], lambda z: own0.at[z], sems_g.at[0], local.at[1]).start()
    gather_pressure(cell, rank, owners, plane, wide, acc, pay1)
    press_z = along_gx(here, lambda x: pay1.at[x], lambda x: hop1.at[x], sems_z.at[1], local.at[2]).start()
    fixed_g.arrive()
    fixed_c = along_col(here, own0, other0, sems_c.at[0]).start()
    press_z.arrive()
    press_g = along_gz(here, lambda z: hop1.at[:, z], lambda z: own1.at[z], sems_g.at[1], local.at[3]).start()
    fixed_c.arrive()
    fixed_rows(col, own0, other0, fixed, rows_ref)
    press_g.arrive()
    press_c = along_col(here, own1, other1, sems_c.at[1]).start()
    press_c.arrive()
    for g in range(GZ):
        press[g] = combine(col, own1[g], other1[g])
    add_loads(press, fixed, rows_ref, acc)
    solve_shell(acc, source, diag, coupling, shell, table)
    pick_answers(table, fixed, rows_ref, answers)
    back_c = along_col(here, answers, other2, sems_c.at[2]).start()
    back_c.arrive()
    for g in range(GZ):
        mixed[g] = combine(col, answers[g], other2[g])
    back_g = along_gz(here, lambda z: mixed.at[z], lambda z: hop2.at[:, z], sems_g.at[2], local.at[4]).start()
    back_g.arrive()
    back_z = along_gx(here, lambda x: hop2.at[x], lambda x: back.at[x], sems_z.at[2], local.at[5]).start()
    back_z.arrive()
    write.wait()
    for stage in (halos, fixed_z, fixed_g, fixed_c, press_z, press_g, press_c, back_c, back_g, back_z):
        stage.sent()


def main_part(owner, node, cell, weight, normal, source, diag, coupling, flux, density, momentum, adjoint, objective):
    hbm = pl.BlockSpec(memory_space=pl.ANY)
    dma = pltpu.SemaphoreType.DMA
    block = (5, CX, CZ, SP)
    return pl.pallas_call(
        main_kernel,
        out_shape=(
            jax.ShapeDtypeStruct((1, FACES), i32),
            jax.ShapeDtypeStruct((CX * CZ, SP), f32),
            jax.ShapeDtypeStruct((64, 3, 128), f32),
            jax.ShapeDtypeStruct((GX, GZ, 128), f32),
            jax.ShapeDtypeStruct(block, f32),
        ),
        in_specs=[vmem()] * 8 + [hbm] * 5,
        out_specs=(vmem(),) * 4 + (hbm,),
        scratch_shapes=[
            pltpu.SMEM((5, 3, 5), f32),
            pltpu.VMEM((CX, CZ, SP), f32),
            pltpu.VMEM((3, CX, CZ, SP), f32),
            pltpu.VMEM(block, f32),
            pltpu.VMEM((5, CX + 4, CZ, SP), f32),
            pltpu.VMEM(block, f32),
            pltpu.VMEM((5, 2, CZ, SP), f32),
            pltpu.VMEM((5, 2, CZ, SP), f32),
            pltpu.VMEM((5, CX, 2, SP), f32),
            pltpu.VMEM((5, CX, 2, SP), f32),
            pltpu.VMEM(block, f32),
            pltpu.VMEM((256, FACES), bf16),
            pltpu.VMEM((256, 128), f32),
            pltpu.VMEM((512, 256), f32),
            pltpu.VMEM((256, 512), bf16),
            pltpu.VMEM((GZ, 256, GX * 128), bf16),
            pltpu.VMEM((192, 256), bf16),
            pltpu.VMEM((4, GX, GZ, 128), f32),
            pltpu.VMEM((GX, 4, GZ, 128), f32),
            pltpu.VMEM((GZ, GX, 4, 128), f32),
            pltpu.VMEM((GZ, GX, 4, 128), f32),
            pltpu.VMEM((GZ, GX, 4, 128), f32),
            pltpu.VMEM((GX, GZ, 128), f32),
            pltpu.VMEM((GX, GZ, 128), f32),
            pltpu.VMEM((GZ, GX, 128), f32),
            pltpu.VMEM((GZ, GX, 128), f32),
            pltpu.VMEM((GZ, GX, 128), f32),
            pltpu.VMEM((GZ, GX, 128), f32),
            pltpu.VMEM((GZ, GX, 128), f32),
            pltpu.VMEM((GZ, GX, 128), f32),
            pltpu.VMEM((GX, GZ, 128), f32),
            dma((2, 5)),
            dma((3, 2, GX - 1)),
            dma((3, 2, GZ - 1)),
            dma((3, 2, 1)),
            dma((6,)),
            dma((6,)),
        ],
        compiler_params=pltpu.CompilerParams(
            collective_id=0, has_side_effects=True, vmem_limit_bytes=VMEM_LIMIT
        ),
        name="main",
    )(owner, node, cell, weight, normal, source, diag, coupling, flux, density, momentum, adjoint, objective)


def update_kernel(
    back, owner_ref, rank_ref, cell_ref, plane_ref, middle, shell, out, shell_out, wide, acc_ref, result, passing, nodes, sems
):
    taken = [
        pltpu.make_async_copy(middle.at[0:4], passing, sems.at[0]),
        pltpu.make_async_copy(shell, nodes, sems.at[1]),
    ]
    given = [
        pltpu.make_async_copy(passing, out.at[0:4], sems.at[2]),
        pltpu.make_async_copy(nodes, shell_out, sems.at[3]),
        pltpu.make_async_copy(result, out.at[4], sems.at[4]),
    ]
    for copy in taken:
        copy.start()
    turned = back[...].reshape(128, 128).T
    high, low = split(jnp.concatenate([turned[0:64], turned[64:128]], 1))
    wide[0:64, :] = high.astype(bf16)
    wide[64:128, :] = low.astype(bf16)
    acc_ref[...] = jnp.zeros_like(acc_ref)

    def face_step(block, _):
        @pl.when(block == 1)
        def _():
            for k in range(2):
                taken[k].wait()
                given[k].start()

        at = pl.ds(pl.multiple_of(block * CHUNK, CHUNK), CHUNK)
        picked = dot(wide[...], as_bf16(one_hot(256, owner_column(owner_ref[:, at]))))
        within = one_hot(64, rank_ref[:, at])
        value = jnp.sum(jnp.where(within, picked[:64] + picked[64:], 0.0), 0, keepdims=True)
        first, second = split(value)
        cell = cell_ref[:, at]
        across = one_hot(SP, cell % SP)
        stacked = jnp.concatenate(
            [jnp.where(across, first, 0.0).astype(bf16), jnp.where(across, second, 0.0).astype(bf16)], 0
        )
        acc_ref[...] += dot_nt(as_bf16(one_hot(CX * CZ, cell // SP)), stacked)
        return 0

    lax.fori_loop(0, FACES // CHUNK, face_step, 0)
    result[...] = (plane_ref[...] + acc_ref[:, :128] + acc_ref[:, 128:]).reshape(CX, CZ, SP)
    given[2].start()
    for copy in given:
        copy.wait()


def update(back, owner, rank, cell, plane, middle, shell):
    hbm = pl.BlockSpec(memory_space=pl.ANY)
    return pl.pallas_call(
        update_kernel,
        out_shape=(
            jax.ShapeDtypeStruct((5, CX, CZ, SP), f32),
            jax.ShapeDtypeStruct((64, 3, 128), f32),
        ),
        in_specs=[vmem()] * 5 + [hbm] * 2,
        out_specs=(hbm, hbm),
        scratch_shapes=[
            pltpu.VMEM((128, 256), bf16),
            pltpu.VMEM((512, 256), f32),
            pltpu.VMEM((CX, CZ, SP), f32),
            pltpu.VMEM((4, CX, CZ, SP), f32),
            pltpu.VMEM((64, 3, 128), f32),
            pltpu.SemaphoreType.DMA((5,)),
        ],
        compiler_params=pltpu.CompilerParams(vmem_limit_bytes=VMEM_LIMIT),
        name="update",
    )(back, owner, rank, cell, plane, middle, shell)


def body(
    density, momentum, adjoint, objective, flux_jac, wall_owner, wall_node, wall_cell,
    wall_weight, wall_normal, shell_source, shell_diag, shell_coupling,
):
    owner = wall_owner.reshape(1, FACES)
    node = wall_node.reshape(1, FACES)
    cell = wall_cell.reshape(1, FACES)
    weight = wall_weight.reshape(1, FACES)
    source = shell_source.reshape(3, 64, 128).transpose(1, 0, 2)
    diag = shell_diag.reshape(3, 64, 128).transpose(1, 0, 2)
    coupling = shell_coupling.reshape(3, 3, 64, 128).transpose(0, 2, 1, 3)
    rank, plane, shell, back, middle = main_part(
        owner, node, cell, weight, wall_normal, source, diag, coupling,
        flux_jac.transpose(1, 0, 2), density, momentum, adjoint, objective,
    )
    fluid_out, shell = update(back, owner, rank, cell, plane, middle, shell)
    return fluid_out, shell.transpose(1, 0, 2).reshape(3, NODES)


def solution(mesh):
    wall = ("gx", "gz", "col")
    return jax.shard_map(
        body,
        mesh=mesh,
        in_specs=(
            P(*wall),
            P(None, *wall),
            P(None, *wall),
            P(None, *wall),
            P(),
            P(wall, None),
            P(wall),
            P(wall),
            P(wall),
            P(None, wall),
            P(None, wall),
            P(None, wall),
            P(None, None, wall),
        ),
        out_specs=(P(None, *wall), P(None, wall)),
        check_vma=False,
    )
```

time: 113 us -> 66 us (0.58)
  Pallas kernels: 110 us -> 65.2 us
  local copies, waits for them, and re-layouts: 1.38 us -> 0 us
    pallas_call x7 -> x2, Pallas kernels: 110 us -> 65.2 us  [the longest x1 59 us: main_part(): pl.pallas_call(main_kernel, out_shape=(jax.ShapeDtypeStruct((1, FACES), i...]
where the time goes in v1:
time: 66 us; the launch traced here: 65.8 us
  Pallas kernels  65.2 us (99%)
    pallas_call x1, Pallas kernels, main_part(): pl.pallas_call(main_kernel, out_shape=(jax.ShapeDtypeStruct((1, FACES), i...  59 us
    pallas_call x1, Pallas kernels, update(): pl.pallas_call(update_kernel, out_shape=(jax.ShapeDtypeStruct((5, CX, CZ,...  6.12 us

profile of v1, /device:TPU:8, one launch (start us, length us, event | category | flops | bytes accessed | tf_op | source)
XLA Modules:
  0.0 65.8 jit_solution(2488118503973401722)
XLA Ops:
  0.6 59.0 %main.1 = (s32[1,8192]{1,0:T(1,128)}, f32[512,128]{1,0:T(8,128)}, f32[64,3,128]{2,1,0:T(4,128)}, f32[8,16,128]{2,1,0:T(8,128)}, f32[5,32,16,128]{3,2,1,0:T(8,128)}) custom-call(s32[1,8192]{1,0:T(1,128)} %bitcast.18, s32[1,8192]{1,0:T(1,128)} %bitcast.24, s32[1,8192]{1,0:T(1,128)} %bitcast.20, f32[1,8192]{1,0:T(1,128)} %bitcast.25, f32[3,8192]{1,0:T(4,128)} %normal.1, ...), custom_call_target="tpu_custom_call" | custom-call | tf_op jit(solution)/shard_map/main/pallas_call | solution.py:419
  59.7 6.1 %update.1 = (f32[5,32,16,128]{3,2,1,0:T(8,128)}, f32[64,3,128]{2,1,0:T(4,128)}) custom-call(f32[8,16,128]{2,1,0:T(8,128)} %get-tuple-element.9.back, s32[1,8192]{1,0:T(1,128)} %bitcast.19, s32[1,8192]{1,0:T(1,128)} %get-tuple-element.10.rank_ref, s32[1,8192]{1,0:T(1,128)} %bitcast.21, f32[512,128]{1,0:T(8,128)} %get-tuple-element.11.plane_ref, ...), custom_call_target="tpu_custom_call" | custom-call | tf_op jit(solution)/shard_map/update/pallas_call | solution.py:525

commit v2 on v1

--- a/solution.py
+++ b/solution.py
@@ -13,6 +13,7 @@
 GX, GZ, COL = 8, 16, 2
 CX, CZ, SP = 32, 16, 128
 FACES, NODES = 8192, 8192
+ZB = 8
 CHUNK = 2048
 VMEM_LIMIT = 56 * 1024 * 1024
 
@@ -154,8 +155,9 @@
     lax.fori_loop(0, FACES // CHUNK, step, 0)
 
 
-def place_fixed(node_ref, weight_ref, normal_ref, rank_ref, owners_ref, acc_ref, pay):
-    acc_ref[...] = jnp.zeros_like(acc_ref)
+def place_fixed(first, last, node_ref, weight_ref, normal_ref, rank_ref, owners_ref, acc_ref):
+    if first == 0:
+        acc_ref[...] = jnp.zeros_like(acc_ref)
 
     def step(block, _):
         at = pl.ds(pl.multiple_of(block * CHUNK, CHUNK), CHUNK)
@@ -172,36 +174,70 @@
         acc_ref[...] += dot_nt(stacked, owners_ref[:, at])
         return 0
 
-    lax.fori_loop(0, FACES // CHUNK, step, 0)
+    lax.fori_loop(first, last, step, 0)
+
+
+def fixed_payload(acc_ref, pay):
     for k in range(4):
         pay[k] = slots_from(
             acc_ref[k * 128 : k * 128 + 64, :] + acc_ref[k * 128 + 64 : k * 128 + 128, :]
         ).reshape(GX, GZ, 128)
 
 
-def stencil(here, flux, density, momentum, adjoint, objective, xlo, xhi, zlo, zhi, side, middle, plane_ref, ext):
+def pack_side(col, ext, packed):
+    lane = lax.broadcasted_iota(i32, (CZ, SP), 1)
+    shift = 2 * (1 - col)
+
+    def step(block, kept):
+        kept = list(kept)
+        for k in range(4):
+            x = block * 4 + k
+            here = (lane // 2) == x
+            for j in range(5):
+                kept[j] = jnp.where(here, pltpu.roll(ext[j, x + 2, ZB : ZB + CZ], 2 * x + shift, 1), kept[j])
+        return tuple(kept)
+
+    kept = lax.fori_loop(0, CX // 4, step, (jnp.zeros((CZ, SP), f32),) * 5)
+    for j in range(5):
+        packed[j] = kept[j]
+
+
+def stencil(here, flux, density, momentum, objective, side, middle, plane_ref, ext):
     gx, gz, col = here
     lane = lax.broadcasted_iota(i32, (CZ, SP), 1)
-    x_low = (gx > 0).astype(f32)
-    x_high = (gx < GX - 1).astype(f32)
-    z_low = (gz > 0).astype(f32)
-    z_high = (gz < GZ - 1).astype(f32)
     s_low = (col > 0).astype(f32)
     s_high = (col < COL - 1).astype(f32)
-    for j in range(5):
-        ext[j, 0:2] = xlo[j] * x_low
-        ext[j, CX + 2 : CX + 4] = xhi[j] * x_high
+    inner = slice(ZB, ZB + CZ)
+    nothing = functools.partial(jnp.zeros, dtype=f32)
+
+    @pl.when(gx == 0)
+    def _():
+        ext[:, 0:2, inner] = nothing((5, 2, CZ, SP))
+
+    @pl.when(gx == GX - 1)
+    def _():
+        ext[:, CX + 2 : CX + 4, inner] = nothing((5, 2, CZ, SP))
+
+    @pl.when(gz == 0)
+    def _():
+        ext[:, 2 : CX + 2, ZB - 2 : ZB] = nothing((5, CX, 2, SP))
+
+    @pl.when(gz == GZ - 1)
+    def _():
+        ext[:, 2 : CX + 2, ZB + CZ : ZB + CZ + 2] = nothing((5, CX, 2, SP))
 
     def one_plane(x):
+        unpack = (2 * SP + 126 * col - 2 * x) % SP
         inverse = (tau / 12.0) / density[x]
         velocity = [momentum[d, x] * inverse for d in range(3)]
         deltas = []
         for j in range(5):
-            now = ext[j, x + 2]
-            beside = side[j, x]
-            dx = 8.0 * (ext[j, x + 1] - ext[j, x + 3]) - (ext[j, x] - ext[j, x + 4])
-            tall = jnp.concatenate([zlo[j, x] * z_low, now, zhi[j, x] * z_high], 0)
-            dz = 8.0 * (tall[1:17] - tall[3:19]) - (tall[0:16] - tall[4:20])
+            now = ext[j, x + 2, inner]
+            beside = pltpu.roll(side[j], unpack, 1)
+            dx = 8.0 * (ext[j, x + 1, inner] - ext[j, x + 3, inner]) - (ext[j, x, inner] - ext[j, x + 4, inner])
+            near = ext[j, x + 2, ZB - 1 : ZB - 1 + CZ] - ext[j, x + 2, ZB + 1 : ZB + 1 + CZ]
+            far = ext[j, x + 2, ZB - 2 : ZB - 2 + CZ] - ext[j, x + 2, ZB + 2 : ZB + 2 + CZ]
+            dz = 8.0 * near - far
             low_side, high_side = beside * s_low, beside * s_high
             ds = 8.0 * (
                 pltpu.roll(jnp.where(lane >= SP - 1, low_side, now), 1, 1)
@@ -216,7 +252,7 @@
             for d in range(3):
                 for j in range(5):
                     total = total + (flux[j, d, i] * (tau / 12.0)) * deltas[j][d]
-            value = ext[i, x + 2] - (total + tau * objective[i, x])
+            value = ext[i, x + 2, inner] - (total + tau * objective[i, x])
             middle[i, x] = value
             if i == 4:
                 plane_ref[pl.ds(pl.multiple_of(x * CZ, CZ), CZ), :] = value
@@ -229,35 +265,44 @@
     lax.fori_loop(0, CX // 2, step, 0)
 
 
-def gather_pressure(cell_ref, rank_ref, owners_ref, plane_ref, wide, acc_ref, pay):
+def cell_rows(cell_ref, cells_ref):
+    def step(block, _):
+        at = pl.ds(pl.multiple_of(block * CHUNK, CHUNK), CHUNK)
+        cells_ref[:, at] = as_bf16(one_hot(CX * CZ, cell_ref[:, at] // SP))
+        return 0
+
+    lax.fori_loop(0, FACES // CHUNK, step, 0)
+
+
+def split_plane(plane_ref, wide, acc_ref):
     high, low = split(plane_ref[...].T)
     wide[0:128, :] = high.astype(bf16)
     wide[128:256, :] = low.astype(bf16)
     acc_ref[0:128, :] = jnp.zeros((128, 256), f32)
 
+
+def gather_pressure(first, last, cell_ref, cells_ref, rank_ref, owners_ref, wide, acc_ref):
     def step(block, _):
         at = pl.ds(pl.multiple_of(block * CHUNK, CHUNK), CHUNK)
-        cell = cell_ref[:, at]
-        picked = dot(wide[...], as_bf16(one_hot(CX * CZ, cell // SP)))
-        across = one_hot(SP, cell % SP)
-        first = jnp.sum(jnp.where(across, picked[:128], 0.0), 0, keepdims=True)
-        second = jnp.sum(jnp.where(across, picked[128:], 0.0), 0, keepdims=True)
+        picked = dot(wide[...], cells_ref[:, at])
+        across = one_hot(SP, cell_ref[:, at] % SP)
+        high = jnp.sum(jnp.where(across, picked[:128], 0.0), 0, keepdims=True)
+        low = jnp.sum(jnp.where(across, picked[128:], 0.0), 0, keepdims=True)
         within = one_hot(64, rank_ref[:, at])
         stacked = jnp.concatenate(
-            [jnp.where(within, first, 0.0).astype(bf16), jnp.where(within, second, 0.0).astype(bf16)], 0
+            [jnp.where(within, high, 0.0).astype(bf16), jnp.where(within, low, 0.0).astype(bf16)], 0
         )
         acc_ref[0:128, :] += dot_nt(stacked, owners_ref[:, at])
         return 0
 
-    lax.fori_loop(0, FACES // CHUNK, step, 0)
+    lax.fori_loop(first, last, step, 0)
+
+
+def pressure_payload(acc_ref, pay):
     pay[...] = slots_from(acc_ref[0:64, :] + acc_ref[64:128, :]).reshape(GX, GZ, 128)
 
 
-ROWS = GX * GZ * 128
-
-
-def flat(ref, *tail):
-    return lambda g: jnp.concatenate([ref[(g, slice(x, x + 1)) + tail] for x in range(GX)], 1)
+WAYS = 4
 
 
 def combine(col, own, other):
@@ -265,18 +310,21 @@
     return jnp.where(half == col, own, pltpu.roll(other, 64, own.ndim - 1))
 
 
-def fixed_rows(col, own, other, fixed, rows_ref):
-    for g in range(GZ):
-        fixed[g] = combine(col, own[g], other[g])
-
-    def step(g, _):
-        for k in range(2):
-            node = row(fixed, 2 * g + k, 3).astype(i32)
+def compact(col, rows, target, first):
+    for h in range(GZ // 2):
+        target[first + h] = combine(col, rows[2 * h + col], rows[2 * h + 1 - col])
+
+
+def fixed_rows(first, last, fixed, rows_ref):
+    def step(h, _):
+        for k in range(WAYS):
+            g = WAYS * h + k
+            node = row(fixed, g, 3).astype(i32)
             line = node // 128
-            rows_ref[2 * g + k] = as_bf16(one_hot(256, (line // 32) * 128 + node % 128))
-        return 0
-
-    lax.fori_loop(0, GZ // 2, step, 0)
+            rows_ref[g] = as_bf16(one_hot(256, (line // 32) * 128 + node % 128))
+        return 0
+
+    lax.fori_loop(first, last, step, 0)
 
 
 def row(fixed, g, k):
@@ -287,13 +335,14 @@
     return one_hot(32, (row(fixed, g, 3).astype(i32) // 128) % 32)
 
 
-def add_loads(press, fixed, rows_ref, acc_ref):
-    acc_ref[0:192, :] = jnp.zeros((192, 256), f32)
+def add_loads(first, last, press, fixed, rows_ref, acc_ref):
+    if first == 0:
+        acc_ref[0:192, :] = jnp.zeros((192, 256), f32)
 
     def step(h, _):
         total = acc_ref[0:192, :]
-        for k in range(2):
-            g = 2 * h + k
+        for k in range(WAYS):
+            g = WAYS * h + k
             columns = node_columns(fixed, g)
             pressure = jnp.concatenate([press[g, x : x + 1, :] for x in range(GX)], 1)
             pieces = []
@@ -304,7 +353,7 @@
         acc_ref[0:192, :] = total
         return 0
 
-    lax.fori_loop(0, GZ // 2, step, 0)
+    lax.fori_loop(first, last, step, 0)
 
 
 def solve_shell(acc_ref, source, diag, coupling, shell_ref, table):
@@ -323,10 +372,10 @@
         table[i * 64 + 32 : i * 64 + 64, :] = low.astype(bf16)
 
 
-def pick_answers(table, fixed, rows_ref, answers):
+def pick_answers(first, last, table, fixed, rows_ref, answers):
     def step(h, _):
-        for k in range(2):
-            g = 2 * h + k
+        for k in range(WAYS):
+            g = WAYS * h + k
             picked = dot(table[...], rows_ref[g])
             columns = node_columns(fixed, g)
             answer = jnp.zeros((1, GX * 128), f32)
@@ -337,77 +386,117 @@
                 answers[g, x : x + 1, :] = answer[:, x * 128 : x * 128 + 128]
         return 0
 
-    lax.fori_loop(0, GZ // 2, step, 0)
+    lax.fori_loop(first, last, step, 0)
+
+
+def mix_answers(col, answers, other, mixed):
+    for h in range(GZ // 2):
+        mixed[2 * h + col] = combine(col, answers[h], other[h])
+        mixed[2 * h + 1 - col] = combine(1 - col, other[h], answers[h])
 
 
 def main_kernel(
-    owner, node, cell, weight, normal, source, diag, coupling,
+    owner, node_hbm, cell_hbm, weight_hbm, normal_hbm, source_hbm, diag_hbm, coupling_hbm,
     flux_hbm, density_hbm, momentum_hbm, adjoint_hbm, objective_hbm,
-    rank, plane, shell, back, middle_hbm,
-    flux, density, momentum, objective, ext, middle, xlo, xhi, zlo, zhi, side,
-    owners, carry, acc, wide, rows_ref, table,
+    back, rank_hbm, plane_hbm, shell_hbm, middle_hbm,
+    node, cell, weight, normal, source, diag, coupling, rank, plane, shell,
+    flux, density, momentum, objective, ext, middle, packed, side,
+    owners, cells, carry, acc, wide, rows_ref, table,
     pay0, hop0, own0, other0, fixed, pay1, hop1, own1, other1, press, answers, other2, mixed, hop2,
-    sems_h, sems_z, sems_g, sems_c, local, loads,
+    sems_h, sems_z, sems_g, sems_c, local, loads, stores,
 ):
     here = gx, gz, col = place()
     greet(gx, gz, col)
     staged = [
-        pltpu.make_async_copy(adjoint_hbm, ext.at[:, 2 : CX + 2], loads.at[0]),
-        pltpu.make_async_copy(momentum_hbm, momentum, loads.at[1]),
-        pltpu.make_async_copy(density_hbm, density, loads.at[2]),
-        pltpu.make_async_copy(objective_hbm, objective, loads.at[3]),
-        pltpu.make_async_copy(flux_hbm, flux, loads.at[4]),
+        pltpu.make_async_copy(source_ref, target, loads.at[k])
+        for k, (source_ref, target) in enumerate(
+            [
+                (adjoint_hbm, ext.at[:, 2 : CX + 2, ZB : ZB + CZ]),
+                (node_hbm, node),
+                (weight_hbm, weight),
+                (normal_hbm, normal),
+                (cell_hbm, cell),
+                (flux_hbm, flux),
+                (density_hbm, density),
+                (momentum_hbm, momentum),
+                (objective_hbm, objective),
+                (source_hbm, source),
+                (diag_hbm, diag),
+                (coupling_hbm, coupling),
+            ]
+        )
     ]
     for copy in staged:
         copy.start()
     rank_faces(owner, rank, owners, carry)
+    staged[0].wait()
+    pack_side(col, ext, packed)
     greeted()
     up, down = ((gx + 1) % GX, gz, col), ((gx + GX - 1) % GX, gz, col)
     high, low = (gx, (gz + 1) % GZ, col), (gx, (gz + GZ - 1) % GZ, col)
+    planes, inner = slice(2, CX + 2), slice(ZB, ZB + CZ)
     halos = Stage(
         [
-            remote(adjoint_hbm.at[:, CX - 2 : CX], xlo, sems_h, 0, up),
-            remote(adjoint_hbm.at[:, 0:2], xhi, sems_h, 1, down),
-            remote(adjoint_hbm.at[:, :, CZ - 2 : CZ], zlo, sems_h, 2, high),
-            remote(adjoint_hbm.at[:, :, 0:2], zhi, sems_h, 3, low),
-            remote(adjoint_hbm, side, sems_h, 4, (gx, gz, 1 - col)),
+            remote(ext.at[:, planes, ZB + CZ - 2 : ZB + CZ], ext.at[:, planes, ZB - 2 : ZB], sems_h, 2, high),
+            remote(ext.at[:, planes, ZB : ZB + 2], ext.at[:, planes, ZB + CZ : ZB + CZ + 2], sems_h, 3, low),
+            remote(ext.at[:, CX : CX + 2, inner], ext.at[:, 0:2, inner], sems_h, 0, up),
+            remote(ext.at[:, 2:4, inner], ext.at[:, CX + 2 : CX + 4, inner], sems_h, 1, down),
+            remote(packed, side, sems_h, 4, (gx, gz, 1 - col)),
         ]
     ).start()
-    place_fixed(node, weight, normal, rank, owners, acc, pay0)
+    for copy in staged[1:]:
+        copy.wait()
+    place_fixed(0, 4, node, weight, normal, rank, owners, acc)
+    fixed_payload(acc, pay0)
     fixed_z = along_gx(here, lambda x: pay0.at[:, x], lambda x: hop0.at[x], sems_z.at[0], local.at[0]).start()
-    for copy in staged:
-        copy.wait()
+    cell_rows(cell, cells)
     halos.arrive()
-    stencil(here, flux, density, momentum, adjoint_hbm, objective, xlo, xhi, zlo, zhi, side, middle, plane, ext)
-    write = pltpu.make_async_copy(middle, middle_hbm, loads.at[5])
-    write.start()
+    stencil(here, flux, density, momentum, objective, side, middle, plane, ext)
+    written = [
+        pltpu.make_async_copy(middle, middle_hbm, stores.at[0]),
+        pltpu.make_async_copy(plane, plane_hbm, stores.at[1]),
+        pltpu.make_async_copy(rank, rank_hbm, stores.at[2]),
+    ]
+    for copy in written:
+        copy.start()
+    split_plane(plane, wide, acc)
+    gather_pressure(0, 3, cell, cells, rank, owners, wide, acc)
     fixed_z.arrive()
     fixed_g = along_gz(here, lambda z: hop0.at[:, :, z], lambda z: own0.at[z], sems_g.at[0], local.at[1]).start()
-    gather_pressure(cell, rank, owners, plane, wide, acc, pay1)
+    gather_pressure(3, 4, cell, cells, rank, owners, wide, acc)
+    pressure_payload(acc, pay1)
     press_z = along_gx(here, lambda x: pay1.at[x], lambda x: hop1.at[x], sems_z.at[1], local.at[2]).start()
+    press_z.arrive()
+    press_g = along_gz(here, lambda z: hop1.at[:, z], lambda z: own1.at[z], sems_g.at[1], local.at[3]).start()
+    half = GZ // WAYS // 2
     fixed_g.arrive()
     fixed_c = along_col(here, own0, other0, sems_c.at[0]).start()
-    press_z.arrive()
-    press_g = along_gz(here, lambda z: hop1.at[:, z], lambda z: own1.at[z], sems_g.at[1], local.at[3]).start()
+    compact(col, own0, fixed, 0)
+    fixed_rows(0, half, fixed, rows_ref)
     fixed_c.arrive()
-    fixed_rows(col, own0, other0, fixed, rows_ref)
+    compact(col, other0, fixed, GZ // 2)
+    fixed_rows(half, 2 * half, fixed, rows_ref)
     press_g.arrive()
     press_c = along_col(here, own1, other1, sems_c.at[1]).start()
+    compact(col, own1, press, 0)
+    add_loads(0, half, press, fixed, rows_ref, acc)
     press_c.arrive()
-    for g in range(GZ):
-        press[g] = combine(col, own1[g], other1[g])
-    add_loads(press, fixed, rows_ref, acc)
+    compact(col, other1, press, GZ // 2)
+    add_loads(half, 2 * half, press, fixed, rows_ref, acc)
     solve_shell(acc, source, diag, coupling, shell, table)
-    pick_answers(table, fixed, rows_ref, answers)
-    back_c = along_col(here, answers, other2, sems_c.at[2]).start()
+    written.append(pltpu.make_async_copy(shell, shell_hbm, stores.at[3]))
+    written[3].start()
+    pick_answers(half, 2 * half, table, fixed, rows_ref, answers)
+    back_c = along_col(here, answers.at[GZ // 2 : GZ], other2, sems_c.at[2]).start()
+    pick_answers(0, half, table, fixed, rows_ref, answers)
     back_c.arrive()
-    for g in range(GZ):
-        mixed[g] = combine(col, answers[g], other2[g])
+    mix_answers(col, answers, other2, mixed)
     back_g = along_gz(here, lambda z: mixed.at[z], lambda z: hop2.at[:, z], sems_g.at[2], local.at[4]).start()
     back_g.arrive()
     back_z = along_gx(here, lambda x: hop2.at[x], lambda x: back.at[x], sems_z.at[2], local.at[5]).start()
     back_z.arrive()
-    write.wait()
+    for copy in written:
+        copy.wait()
     for stage in (halos, fixed_z, fixed_g, fixed_c, press_z, press_g, press_c, back_c, back_g, back_z):
         stage.sent()
 
@@ -419,27 +508,35 @@
     return pl.pallas_call(
         main_kernel,
         out_shape=(
+            jax.ShapeDtypeStruct((GX, GZ, 128), f32),
             jax.ShapeDtypeStruct((1, FACES), i32),
             jax.ShapeDtypeStruct((CX * CZ, SP), f32),
             jax.ShapeDtypeStruct((64, 3, 128), f32),
-            jax.ShapeDtypeStruct((GX, GZ, 128), f32),
             jax.ShapeDtypeStruct(block, f32),
         ),
-        in_specs=[vmem()] * 8 + [hbm] * 5,
-        out_specs=(vmem(),) * 4 + (hbm,),
+        in_specs=[vmem()] + [hbm] * 12,
+        out_specs=(vmem(),) + (hbm,) * 4,
         scratch_shapes=[
+            pltpu.VMEM((1, FACES), i32),
+            pltpu.VMEM((1, FACES), i32),
+            pltpu.VMEM((1, FACES), f32),
+            pltpu.VMEM((3, FACES), f32),
+            pltpu.VMEM((64, 3, 128), f32),
+            pltpu.VMEM((64, 3, 128), f32),
+            pltpu.VMEM((3, 64, 3, 128), f32),
+            pltpu.VMEM((1, FACES), i32),
+            pltpu.VMEM((CX * CZ, SP), f32),
+            pltpu.VMEM((64, 3, 128), f32),
             pltpu.SMEM((5, 3, 5), f32),
             pltpu.VMEM((CX, CZ, SP), f32),
             pltpu.VMEM((3, CX, CZ, SP), f32),
             pltpu.VMEM(block, f32),
-            pltpu.VMEM((5, CX + 4, CZ, SP), f32),
+            pltpu.VMEM((5, CX + 4, 2 * ZB + CZ, SP), f32),
             pltpu.VMEM(block, f32),
-            pltpu.VMEM((5, 2, CZ, SP), f32),
-            pltpu.VMEM((5, 2, CZ, SP), f32),
-            pltpu.VMEM((5, CX, 2, SP), f32),
-            pltpu.VMEM((5, CX, 2, SP), f32),
-            pltpu.VMEM(block, f32),
+            pltpu.VMEM((5, CZ, SP), f32),
+            pltpu.VMEM((5, CZ, SP), f32),
             pltpu.VMEM((256, FACES), bf16),
+            pltpu.VMEM((CX * CZ, FACES), bf16),
             pltpu.VMEM((256, 128), f32),
             pltpu.VMEM((512, 256), f32),
             pltpu.VMEM((256, 512), bf16),
@@ -456,7 +553,7 @@
             pltpu.VMEM((GZ, GX, 128), f32),
             pltpu.VMEM((GZ, GX, 128), f32),
             pltpu.VMEM((GZ, GX, 128), f32),
-            pltpu.VMEM((GZ, GX, 128), f32),
+            pltpu.VMEM((GZ // 2, GX, 128), f32),
             pltpu.VMEM((GZ, GX, 128), f32),
             pltpu.VMEM((GX, GZ, 128), f32),
             dma((2, 5)),
@@ -464,7 +561,8 @@
             dma((3, 2, GZ - 1)),
             dma((3, 2, 1)),
             dma((6,)),
-            dma((6,)),
+            dma((12,)),
+            dma((4,)),
         ],
         compiler_params=pltpu.CompilerParams(
             collective_id=0, has_side_effects=True, vmem_limit_bytes=VMEM_LIMIT
@@ -554,7 +652,7 @@
     source = shell_source.reshape(3, 64, 128).transpose(1, 0, 2)
     diag = shell_diag.reshape(3, 64, 128).transpose(1, 0, 2)
     coupling = shell_coupling.reshape(3, 3, 64, 128).transpose(0, 2, 1, 3)
-    rank, plane, shell, back, middle = main_part(
+    back, rank, plane, shell, middle = main_part(
         owner, node, cell, weight, wall_normal, source, diag, coupling,
         flux_jac.transpose(1, 0, 2), density, momentum, adjoint, objective,
     )

time: 66 us -> 62.3 us (0.944)
  Pallas kernels: 65.2 us -> 61.2 us
    pallas_call x1, Pallas kernels: 59 us -> 55.1 us  [main_part(): pl.pallas_call(main_kernel, out_shape=(jax.ShapeDtypeStruct((GX, GZ, 128)...]
where the time goes in v2:
time: 62.3 us; the launch traced here: 61.9 us
  Pallas kernels  61.2 us (98%)
  between operations  0.64 us (1%)
    pallas_call x1, Pallas kernels, main_part(): pl.pallas_call(main_kernel, out_shape=(jax.ShapeDtypeStruct((GX, GZ, 128)...  55.1 us
    pallas_call x1, Pallas kernels, update(): pl.pallas_call(update_kernel, out_shape=(jax.ShapeDtypeStruct((5, CX, CZ,...  6.12 us

profile of v2, /device:TPU:8, one launch (start us, length us, event | category | flops | bytes accessed | tf_op | source)
XLA Modules:
  0.0 61.9 jit_solution(4138545306865714091)
XLA Ops:
  0.6 55.1 %main.1 = (f32[8,16,128]{2,1,0:T(8,128)}, s32[1,8192]{1,0:T(1,128)}, f32[512,128]{1,0:T(8,128)}, f32[64,3,128]{2,1,0:T(4,128)}, f32[5,32,16,128]{3,2,1,0:T(8,128)}) custom-call(s32[1,8192]{1,0:T(1,128)} %bitcast.18, s32[1,8192]{1,0:T(1,128)} %bitcast.24, s32[1,8192]{1,0:T(1,128)} %bitcast.20, f32[1,8192]{1,0:T(1,128)} %bitcast.25, f32[3,8192]{1,0:T(4,128)} %normal_hbm.1, ...), custom_call_target="tpu_custom_call" | custom-call | tf_op jit(solution)/shard_map/main/pallas_call | solution.py:508
  55.8 6.1 %update.1 = (f32[5,32,16,128]{3,2,1,0:T(8,128)}, f32[64,3,128]{2,1,0:T(4,128)}) custom-call(f32[8,16,128]{2,1,0:T(8,128)} %get-tuple-element.9.back, s32[1,8192]{1,0:T(1,128)} %bitcast.19, s32[1,8192]{1,0:T(1,128)} %get-tuple-element.10.rank_ref, s32[1,8192]{1,0:T(1,128)} %bitcast.21, f32[512,128]{1,0:T(8,128)} %get-tuple-element.11.plane_ref, ...), custom_call_target="tpu_custom_call" | custom-call | tf_op jit(solution)/shard_map/update/pallas_call | solution.py:623

commit v3 on v2

--- a/solution.py
+++ b/solution.py
@@ -22,6 +22,10 @@
     return pl.BlockSpec(memory_space=pltpu.VMEM)
 
 
+def part(block):
+    return pl.ds(pl.multiple_of(block * CHUNK, CHUNK), CHUNK)
+
+
 def split(x):
     high = x.astype(bf16).astype(f32)
     return high, x - high
@@ -135,7 +139,7 @@
     carry_ref[...] = jnp.zeros_like(carry_ref)
 
     def step(block, _):
-        at = pl.ds(pl.multiple_of(block * CHUNK, CHUNK), CHUNK)
+        at = part(block)
         mask = one_hot(256, owner_column(owner_ref[:, at]))
         chosen = as_bf16(mask)
         owners_ref[:, at] = chosen
@@ -160,7 +164,7 @@
         acc_ref[...] = jnp.zeros_like(acc_ref)
 
     def step(block, _):
-        at = pl.ds(pl.multiple_of(block * CHUNK, CHUNK), CHUNK)
+        at = part(block)
         within = one_hot(64, rank_ref[:, at])
         weight = weight_ref[:, at]
         node = node_ref[:, at]
@@ -186,20 +190,13 @@
 
 def pack_side(col, ext, packed):
     lane = lax.broadcasted_iota(i32, (CZ, SP), 1)
-    shift = 2 * (1 - col)
-
-    def step(block, kept):
-        kept = list(kept)
-        for k in range(4):
-            x = block * 4 + k
-            here = (lane // 2) == x
-            for j in range(5):
-                kept[j] = jnp.where(here, pltpu.roll(ext[j, x + 2, ZB : ZB + CZ], 2 * x + shift, 1), kept[j])
-        return tuple(kept)
-
-    kept = lax.fori_loop(0, CX // 4, step, (jnp.zeros((CZ, SP), f32),) * 5)
+    lane = (lane + 2 + 126 * col) % SP
     for j in range(5):
-        packed[j] = kept[j]
+        kept = ext[j, 2, ZB : ZB + CZ]
+        for x in range(1, CX):
+            moved = pltpu.roll(ext[j, x + 2, ZB : ZB + CZ], 2 * x, 1)
+            kept = jnp.where(lane // 2 == x, moved, kept)
+        packed[j] = kept
 
 
 def stencil(here, flux, density, momentum, objective, side, middle, plane_ref, ext):
@@ -226,52 +223,44 @@
     def _():
         ext[:, 2 : CX + 2, ZB + CZ : ZB + CZ + 2] = nothing((5, CX, 2, SP))
 
-    def one_plane(x):
-        unpack = (2 * SP + 126 * col - 2 * x) % SP
-        inverse = (tau / 12.0) / density[x]
+    def one_plane(x, sides):
+        inverse = 1.0 / density[x]
         velocity = [momentum[d, x] * inverse for d in range(3)]
-        deltas = []
+        totals = [12.0 * objective[i, x] for i in range(5)]
         for j in range(5):
             now = ext[j, x + 2, inner]
-            beside = pltpu.roll(side[j], unpack, 1)
-            dx = 8.0 * (ext[j, x + 1, inner] - ext[j, x + 3, inner]) - (ext[j, x, inner] - ext[j, x + 4, inner])
+            near = ext[j, x + 1, inner] - ext[j, x + 3, inner]
+            far = ext[j, x, inner] - ext[j, x + 4, inner]
+            spread(totals, velocity, j, 0, 8.0 * near - far)
             near = ext[j, x + 2, ZB - 1 : ZB - 1 + CZ] - ext[j, x + 2, ZB + 1 : ZB + 1 + CZ]
             far = ext[j, x + 2, ZB - 2 : ZB - 2 + CZ] - ext[j, x + 2, ZB + 2 : ZB + 2 + CZ]
-            dz = 8.0 * near - far
-            low_side, high_side = beside * s_low, beside * s_high
-            ds = 8.0 * (
-                pltpu.roll(jnp.where(lane >= SP - 1, low_side, now), 1, 1)
-                - pltpu.roll(jnp.where(lane < 1, high_side, now), SP - 1, 1)
-            ) - (
-                pltpu.roll(jnp.where(lane >= SP - 2, low_side, now), 2, 1)
-                - pltpu.roll(jnp.where(lane < 2, high_side, now), SP - 2, 1)
+            spread(totals, velocity, j, 1, 8.0 * near - far)
+            low_side, high_side = sides[j] * s_low, sides[j] * s_high
+            near = pltpu.roll(jnp.where(lane >= SP - 1, low_side, now), 1, 1) - pltpu.roll(
+                jnp.where(lane < 1, high_side, now), SP - 1, 1
             )
-            deltas.append((dx, dz, ds))
+            far = pltpu.roll(jnp.where(lane >= SP - 2, low_side, now), 2, 1) - pltpu.roll(
+                jnp.where(lane < 2, high_side, now), SP - 2, 1
+            )
+            spread(totals, velocity, j, 2, 8.0 * near - far)
         for i in range(5):
-            total = velocity[0] * deltas[i][0] + velocity[1] * deltas[i][1] + velocity[2] * deltas[i][2]
-            for d in range(3):
-                for j in range(5):
-                    total = total + (flux[j, d, i] * (tau / 12.0)) * deltas[j][d]
-            value = ext[i, x + 2, inner] - (total + tau * objective[i, x])
+            value = ext[i, x + 2, inner] - (tau / 12.0) * totals[i]
             middle[i, x] = value
             if i == 4:
                 plane_ref[pl.ds(pl.multiple_of(x * CZ, CZ), CZ), :] = value
 
-    def step(x, _):
-        for k in range(2):
-            one_plane(2 * x + k)
-        return 0
-
-    lax.fori_loop(0, CX // 2, step, 0)
-
-
-def cell_rows(cell_ref, cells_ref):
-    def step(block, _):
-        at = pl.ds(pl.multiple_of(block * CHUNK, CHUNK), CHUNK)
-        cells_ref[:, at] = as_bf16(one_hot(CX * CZ, cell_ref[:, at] // SP))
-        return 0
-
-    lax.fori_loop(0, FACES // CHUNK, step, 0)
+    def spread(totals, velocity, j, d, delta):
+        totals[j] = totals[j] + velocity[d] * delta
+        for i in range(5):
+            totals[i] = totals[i] + flux[j, d, i] * delta
+
+    def step(block, sides):
+        for k in range(PLANES):
+            one_plane(PLANES * block + k, sides)
+            sides = tuple(pltpu.roll(value, SP - 2, 1) for value in sides)
+        return sides
+
+    lax.fori_loop(0, CX // PLANES, step, tuple(side[j] for j in range(5)))
 
 
 def split_plane(plane_ref, wide, acc_ref):
@@ -281,10 +270,10 @@
     acc_ref[0:128, :] = jnp.zeros((128, 256), f32)
 
 
-def gather_pressure(first, last, cell_ref, cells_ref, rank_ref, owners_ref, wide, acc_ref):
+def gather_pressure(first, last, cell_ref, rank_ref, owners_ref, wide, acc_ref):
     def step(block, _):
-        at = pl.ds(pl.multiple_of(block * CHUNK, CHUNK), CHUNK)
-        picked = dot(wide[...], cells_ref[:, at])
+        at = part(block)
+        picked = dot(wide[...], as_bf16(one_hot(CX * CZ, cell_ref[:, at] // SP)))
         across = one_hot(SP, cell_ref[:, at] % SP)
         high = jnp.sum(jnp.where(across, picked[:128], 0.0), 0, keepdims=True)
         low = jnp.sum(jnp.where(across, picked[128:], 0.0), 0, keepdims=True)
@@ -302,7 +291,8 @@
     pay[...] = slots_from(acc_ref[0:64, :] + acc_ref[64:128, :]).reshape(GX, GZ, 128)
 
 
-WAYS = 4
+WAYS = 2
+PLANES = 2
 
 
 def combine(col, own, other):
@@ -401,7 +391,7 @@
     back, rank_hbm, plane_hbm, shell_hbm, middle_hbm,
     node, cell, weight, normal, source, diag, coupling, rank, plane, shell,
     flux, density, momentum, objective, ext, middle, packed, side,
-    owners, cells, carry, acc, wide, rows_ref, table,
+    owners, carry, acc, wide, rows_ref, table,
     pay0, hop0, own0, other0, fixed, pay1, hop1, own1, other1, press, answers, other2, mixed, hop2,
     sems_h, sems_z, sems_g, sems_c, local, loads, stores,
 ):
@@ -449,7 +439,6 @@
     place_fixed(0, 4, node, weight, normal, rank, owners, acc)
     fixed_payload(acc, pay0)
     fixed_z = along_gx(here, lambda x: pay0.at[:, x], lambda x: hop0.at[x], sems_z.at[0], local.at[0]).start()
-    cell_rows(cell, cells)
     halos.arrive()
     stencil(here, flux, density, momentum, objective, side, middle, plane, ext)
     written = [
@@ -460,10 +449,10 @@
     for copy in written:
         copy.start()
     split_plane(plane, wide, acc)
-    gather_pressure(0, 3, cell, cells, rank, owners, wide, acc)
+    gather_pressure(0, 3, cell, rank, owners, wide, acc)
     fixed_z.arrive()
     fixed_g = along_gz(here, lambda z: hop0.at[:, :, z], lambda z: own0.at[z], sems_g.at[0], local.at[1]).start()
-    gather_pressure(3, 4, cell, cells, rank, owners, wide, acc)
+    gather_pressure(3, 4, cell, rank, owners, wide, acc)
     pressure_payload(acc, pay1)
     press_z = along_gx(here, lambda x: pay1.at[x], lambda x: hop1.at[x], sems_z.at[1], local.at[2]).start()
     press_z.arrive()
@@ -536,7 +525,6 @@
             pltpu.VMEM((5, CZ, SP), f32),
             pltpu.VMEM((5, CZ, SP), f32),
             pltpu.VMEM((256, FACES), bf16),
-            pltpu.VMEM((CX * CZ, FACES), bf16),
             pltpu.VMEM((256, 128), f32),
             pltpu.VMEM((512, 256), f32),
             pltpu.VMEM((256, 512), bf16),
@@ -598,7 +586,7 @@
                 taken[k].wait()
                 given[k].start()
 
-        at = pl.ds(pl.multiple_of(block * CHUNK, CHUNK), CHUNK)
+        at = part(block)
         picked = dot(wide[...], as_bf16(one_hot(256, owner_column(owner_ref[:, at]))))
         within = one_hot(64, rank_ref[:, at])
         value = jnp.sum(jnp.where(within, picked[:64] + picked[64:], 0.0), 0, keepdims=True)

time: 62.3 us -> 61.7 us (level)
  no operation moved by 1% of the time
where the time goes in v3:
time: 61.7 us; the launch traced here: 61.5 us
  Pallas kernels  60.9 us (99%)
  between operations  0.64 us (1%)
    pallas_call x1, Pallas kernels, main_part(): pl.pallas_call(main_kernel, out_shape=(jax.ShapeDtypeStruct((GX, GZ, 128)...  54.8 us
    pallas_call x1, Pallas kernels, update(): pl.pallas_call(update_kernel, out_shape=(jax.ShapeDtypeStruct((5, CX, CZ,...  6.12 us

profile of v3, /device:TPU:8, one launch (start us, length us, event | category | flops | bytes accessed | tf_op | source)
XLA Modules:
  0.0 61.5 jit_solution(8002486238597126452)
XLA Ops:
  0.6 54.8 %main.1 = (f32[8,16,128]{2,1,0:T(8,128)}, s32[1,8192]{1,0:T(1,128)}, f32[512,128]{1,0:T(8,128)}, f32[64,3,128]{2,1,0:T(4,128)}, f32[5,32,16,128]{3,2,1,0:T(8,128)}) custom-call(s32[1,8192]{1,0:T(1,128)} %bitcast.18, s32[1,8192]{1,0:T(1,128)} %bitcast.24, s32[1,8192]{1,0:T(1,128)} %bitcast.20, f32[1,8192]{1,0:T(1,128)} %bitcast.25, f32[3,8192]{1,0:T(4,128)} %normal_hbm.1, ...), custom_call_target="tpu_custom_call" | custom-call | tf_op jit(solution)/shard_map/main/pallas_call | solution.py:497
  55.4 6.1 %update.1 = (f32[5,32,16,128]{3,2,1,0:T(8,128)}, f32[64,3,128]{2,1,0:T(4,128)}) custom-call(f32[8,16,128]{2,1,0:T(8,128)} %get-tuple-element.9.back, s32[1,8192]{1,0:T(1,128)} %bitcast.19, s32[1,8192]{1,0:T(1,128)} %get-tuple-element.10.rank_ref, s32[1,8192]{1,0:T(1,128)} %bitcast.21, f32[512,128]{1,0:T(8,128)} %get-tuple-element.11.plane_ref, ...), custom_call_target="tpu_custom_call" | custom-call | tf_op jit(solution)/shard_map/update/pallas_call | solution.py:611
